TPU v7x, 32 devices: a whole 2x2x4 slice. The times are simulated.
32 devices in a mesh: grp: 16 (over z, y, core), dev: 2 (over x).
Axes of the slice: x: 2, y: 2, z: 4, core: 2. Of those that a mesh axis runs over, the one named last changes fastest.
Arguments:
- operators: bfloat16 [64, 1024, 1024], P(('grp', 'dev')), may hold values from -0.3 to 2.3, as said below
- forces: float32 [64, 32, 512], P(('grp', 'dev')), may hold values from -48 to 48
- weights: float32 [64, 512], P(('grp', 'dev')), may hold values from 0.5 to 2
- lengths: int32 [64], replicated, may hold values from 128 to 512, as said below
- slot_order: int32 [64, 512], P(('grp', 'dev')), may hold values from 0 to 511, as said below
Outputs:
- solution: float32 [64, 32, 512], P(('grp', 'dev'))
- residual: float32 [64, 32, 512], P(('grp', 'dev'))
Inputs may be any that keep to these rules, and one draw needn't show every extreme that they name: `lengths`: every interface has at least 128 live multipliers and some interface has exactly 512; the last entry belongs to the end of the chain and is not used. `slot_order`: row k is a permutation of 0 to 511 that maps the first lengths[k] positions onto the first lengths[k] slots and leaves the other positions in place. `operators`: each operator is symmetric, and positive definite on every subset of its rows and columns.
All inputs are finite; a program needn't handle non-finite values.
Results may differ from a plain program's by a relative error of at most 0.01.
Values may be sent and summed in bfloat16 or wider, within the bound.
A program may use at most 64 MiB of HBM per device.

v0:
```python
import functools

import jax
import jax.numpy as jnp
from jax import lax
from jax.experimental import pallas as pl
from jax.experimental.pallas import tpu as pltpu
from jax.sharding import PartitionSpec as P

MESH = pl.DeviceIdType.MESH
F32, BF16 = jnp.float32, jnp.bfloat16
EXACT = lax.Precision.HIGHEST


def plan_stages(groups, devs):
    factors = []
    while groups > 1:
        factor = next((f for f in (4, 3, 2, 5, 7) if groups % f == 0), groups)
        factors.append(factor)
        groups //= factor
    first = factors[0] if factors else 1
    stages, stride = [(devs * first, None, first)], first
    for factor in factors[1:]:
        stages.append((factor, stride, factor))
        stride *= factor
    return [stage for stage in stages if stage[0] > 1]


def peer(stage, offset, grp, dev, devs):
    size, stride, factor = stage
    if stride is None:
        low = lax.rem(grp, factor)
        place = lax.rem(low * devs + dev + offset, size)
        return grp - low + lax.div(place, devs), lax.rem(place, devs)
    digit = lax.rem(lax.div(grp, stride), factor)
    return grp + (lax.rem(digit + offset, factor) - digit) * stride, dev


def split(x):
    high = x.astype(BF16)
    return high, (x - high.astype(F32)).astype(BF16)


def dot(x, y):
    return jnp.dot(x, y, preferred_element_type=F32)


def dot_nt(x, y, precision=None):
    return lax.dot_general(
        x, y, (((1,), (1,)), ((), ())), precision=precision, preferred_element_type=F32
    )


def small(x, y):
    return jnp.dot(x, y, precision=EXACT, preferred_element_type=F32)


def small_tn(x, y):
    return lax.dot_general(
        x, y, (((0,), (0,)), ((), ())), precision=EXACT, preferred_element_type=F32
    )


def pack(matrix):
    size = matrix.shape[0]
    parts = max(1, min(128 // size, size // 8))
    rows = size // parts
    return jnp.concatenate([matrix[i * rows : (i + 1) * rows] for i in range(parts)], axis=1)


def unpack(packed, size):
    parts = packed.shape[1] // size
    return jnp.concatenate([packed[:, i * size : (i + 1) * size] for i in range(parts)], axis=0)


def eliminate(matrix, targets, between=None):
    size = matrix.shape[0]
    held = jnp.concatenate([matrix, targets], axis=1)
    width = held.shape[1]
    index = lax.broadcasted_iota(jnp.int32, (size, 1), 0)
    block = 4 if size % 4 == 0 else 1
    for p in range(0, size, block):
        if between is not None and p == size // 2:
            between()
        rows = [held[p + i : p + i + 1, :] for i in range(block)]
        entries = [
            [jnp.broadcast_to(row[:, p + j : p + j + 1], (1, width)) for j in range(block)] for row in rows
        ]
        columns = [held[:, p + j : p + j + 1] for j in range(block)]
        for i in range(block):
            scale = 1.0 / entries[i][i]
            rows[i] = rows[i] * scale
            entries[i] = [entry * scale for entry in entries[i]]
            for k in range(block):
                if k != i:
                    factor = entries[k][i]
                    rows[k] = rows[k] - factor * rows[i]
                    entries[k] = [a - factor * b for a, b in zip(entries[k], entries[i])]
        update = columns[0] * rows[0]
        for j in range(1, block):
            update = update + columns[j] * rows[j]
        held = held - update
        for j in range(block):
            held = jnp.where(index == p + j, rows[j], held)
    return held[:, size:]


def kernel(stages, devs, total, lengths_hbm, forces_hbm, weights_hbm, order_hbm, operators_ref,
           solution_ref, residual_ref,
           lengths_ref, forces_ref, weights_ref, order_ref, ops, pick, start, search, image, remainder, scaled, second, product,
           fwd_src, fwd_dst, fwd2_src, fwd2_dst, ret_src, ret_dst, retlow_src, retlow_dst,
           ret2_src, ret2_dst, sums_src, sums_dst, last_src, last_dst,
           ops_sem, small_sem, halo_send, halo_recv, sums_send, sums_recv, last_send, last_recv):
    number, loads, breadth = forces_ref.shape
    grp, dev = lax.axis_index("grp"), lax.axis_index("dev")
    me = grp * devs + dev
    has_prev, has_next = me > 0, me < total - 1
    before, after = jnp.maximum(me - 1, 0), jnp.minimum(me + 1, total - 1)
    prev_id = (lax.div(before, devs), lax.rem(before, devs))
    next_id = (lax.div(after, devs), lax.rem(after, devs))

    barrier = pltpu.get_barrier_semaphore()
    partners = 0
    for stage in stages:
        for offset in range(1, stage[0]):
            pl.semaphore_signal(barrier, inc=1, device_id=peer(stage, offset, grp, dev, devs), device_id_type=MESH)
            partners += 1

    @pl.when(has_prev)
    def _():
        pl.semaphore_signal(barrier, inc=1, device_id=prev_id, device_id_type=MESH)

    @pl.when(has_next)
    def _():
        pl.semaphore_signal(barrier, inc=1, device_id=next_id, device_id_type=MESH)

    fetching = [
        pltpu.make_async_copy(source, target, small_sem.at[i])
        for i, (source, target) in enumerate((
            (order_hbm, order_ref), (forces_hbm, forces_ref), (weights_hbm, weights_ref), (lengths_hbm, lengths_ref),
        ))
    ]
    for copy in fetching:
        copy.start()
    loading = [pltpu.make_async_copy(operators_ref.at[l], ops.at[l], ops_sem.at[l]) for l in range(number)]
    for copy in loading:
        copy.start()

    def remote(slot, source, target, where):
        return pltpu.make_async_remote_copy(
            src_ref=source, dst_ref=target, send_sem=halo_send.at[slot], recv_sem=halo_recv.at[slot],
            device_id=where, device_id_type=MESH,
        )

    forward = remote(0, fwd_src.at[0], fwd_dst.at[0], next_id)
    forward_low = remote(1, fwd_src.at[1], fwd_dst.at[1], next_id)
    forward_second = remote(2, fwd2_src, fwd2_dst, next_id)
    back = remote(3, ret_src, ret_dst, prev_id)
    back_low = remote(4, retlow_src, retlow_dst, prev_id)
    back_second = remote(5, ret2_src, ret2_dst, prev_id)

    def start_if(condition, *copies):
        @pl.when(condition)
        def _():
            for copy in copies:
                copy.start()

    def arrived(condition, copy, buffer):
        @pl.when(condition)
        def _():
            copy.wait_recv()

        @pl.when(jnp.logical_not(condition))
        def _():
            buffer[...] = jnp.zeros_like(buffer)

    for copy in fetching:
        copy.wait()
    positions = lax.broadcasted_iota(jnp.int32, (1, breadth), 1)
    masks = []
    for l in range(number):
        k = me * number + l
        live = jnp.where(k < total * number - 1, lengths_ref[k], 0)
        masks.append(positions < live)
    slots = lax.broadcasted_iota(jnp.int32, (breadth, breadth), 0)

    turned = [None] * number
    stacks = [None] * number
    for l in reversed(range(number)):
        pick[l] = jnp.where(slots == order_ref[l : l + 1, :], 1.0, 0.0).astype(BF16)
        start[l] = jnp.where(masks[l], forces_ref[l], 0.0)
        search[l] = start[l] * weights_ref[l : l + 1, :]
        high, low = split(search[l])
        stacks[l] = jnp.concatenate([high, low], axis=0)
        turned[l] = dot(stacks[l], pick[l]).astype(BF16)
        if l == number - 1:
            fwd_src[0] = turned[l][:loads]
            fwd_src[1] = turned[l][loads:]
            pl.semaphore_wait(barrier, partners + has_prev.astype(jnp.int32) + has_next.astype(jnp.int32))
            start_if(has_next, forward, forward_low)

    for copy in loading:
        copy.wait()

    def own_products(stacks, turned):
        product[0] = dot(stacks[0], ops[0, breadth:, :])
        for l in range(1, number):
            product[l] = dot(jnp.concatenate([turned[l - 1], stacks[l]], axis=1), ops[l])

    def gather(l, field):
        high, low = split(field)
        both = dot_nt(jnp.concatenate([high, low], axis=0), pick[l])
        return both[:loads] + both[loads:]

    own_products(stacks, turned)
    arrived(has_prev, forward, fwd_dst.at[0])
    ret_src[...] = product[0, :loads, :breadth] + dot(fwd_dst[0], ops[0, :breadth, :breadth])
    start_if(has_prev, back)
    product[0, :loads, breadth:] += dot(fwd_dst[0], ops[0, :breadth, breadth:])
    arrived(has_prev, forward_low, fwd_dst.at[1])
    product[0, loads:, :] += dot(fwd_dst[1], ops[0, :breadth, :])
    retlow_src[...] = product[0, loads:, :breadth].astype(BF16)
    start_if(has_prev, back_low)

    def finish_image(l, left):
        image[l] = jnp.where(masks[l], product[l, :loads, breadth:] + gather(l, left), 0.0)
        scaled[l] = weights_ref[l : l + 1, :] * image[l]
        high, low = split(scaled[l])
        stacks[l] = jnp.concatenate([high, low], axis=0)
        turned[l] = dot(stacks[l], pick[l]).astype(BF16)

    def gram(l):
        pair = dot_nt(jnp.concatenate([search[l], scaled[l]], axis=0), image[l], EXACT)
        return pair[:loads], pair[loads:]

    curvature = projection = middle = 0.0
    for l in range(number):
        remainder[l] = product[l, loads:, breadth:]
        projection = projection + dot_nt(search[l], start[l], EXACT)
        if l < number - 1:
            finish_image(l, product[l + 1, :loads, :breadth])
            remainder[l] += dot_nt(product[l + 1, loads:, :breadth].astype(BF16), pick[l])
            first, second_part = gram(l)
            curvature, middle = curvature + first, middle + second_part
    arrived(has_next, back, ret_dst)
    finish_image(number - 1, ret_dst[...])
    fwd2_src[...] = turned[number - 1]
    start_if(has_next, forward_second)
    first, second_part = gram(number - 1)
    curvature, middle = curvature + first, middle + second_part

    def exchange(s, source, inbox, send_sem, recv_sem):
        copies = []
        for offset in range(1, stages[s][0]):
            place = sum(stage[0] - 1 for stage in stages[:s]) + offset - 1
            copies.append(pltpu.make_async_remote_copy(
                src_ref=source.at[s], dst_ref=inbox.at[place], send_sem=send_sem.at[place],
                recv_sem=recv_sem.at[place], device_id=peer(stages[s], offset, grp, dev, devs),
                device_id_type=MESH,
            ))
            copies[-1].start()
        return copies

    def collect(s, copies, source, inbox):
        first = sum(stage[0] - 1 for stage in stages[:s])
        value = source[s]
        for i, copy in enumerate(copies):
            copy.wait_recv()
            value = value + inbox[first + i]
        return value

    tall = pack(curvature).shape[0]
    sums_src[0] = jnp.concatenate([pack(curvature), pack(projection), pack(middle)], axis=0)
    pending = [exchange(0, sums_src, sums_dst, sums_send, sums_recv)]

    own_products(stacks, turned)

    def energy(pair, values):
        return dot_nt(pair[:loads].astype(F32) + pair[loads:].astype(F32), values[:loads] + values[loads:], EXACT)

    outer = 0.0
    for l in range(number):
        outer = outer + energy(stacks[l], product[l, :, breadth:])
        if l > 0:
            outer = outer + energy(turned[l - 1], product[l, :, :breadth])
    for s in range(1, len(stages)):
        sums_src[s] = collect(s - 1, pending[-1], sums_src, sums_dst)
        pending.append(exchange(s, sums_src, sums_dst, sums_send, sums_recv))
    arrived(has_prev, forward_second, fwd2_dst)
    left_own = product[0, :, :breadth]
    left_extra = dot(fwd2_dst[...], ops[0, :breadth, :breadth])
    mixed = energy(fwd2_dst[...], left_extra + 2.0 * left_own)
    outer = outer + mixed
    last_src[0] = pack(outer)
    trailing = [exchange(0, last_src, last_dst, last_send, last_recv)]
    left_total = left_own + left_extra
    ret2_src[...] = left_total[:loads] + left_total[loads:]
    start_if(has_prev, back_second)
    product[0, :, breadth:] += dot(fwd2_dst[...], ops[0, :breadth, breadth:])

    def advance():
        for s in range(1, len(stages)):
            last_src[s] = collect(s - 1, trailing[-1], last_src, last_dst)
            trailing.append(exchange(s, last_src, last_dst, last_send, last_recv))

    summed = collect(len(stages) - 1, pending[-1], sums_src, sums_dst)
    curvature = unpack(summed[:tall], loads)
    projection = unpack(summed[tall : 2 * tall], loads)
    middle = unpack(summed[2 * tall :], loads)
    solved = eliminate(curvature, jnp.concatenate([projection, middle], axis=1), advance)
    alpha = solved[:, :loads]
    shift = small(solved[:, loads:], alpha)
    right_side = small_tn(alpha, small(middle, alpha) - curvature)
    known = small(middle, shift)
    for l in range(number):
        right = product[l, :loads, breadth:] + product[l, loads:, breadth:]
        if l < number - 1:
            left = product[l + 1, :loads, :breadth] + product[l + 1, loads:, :breadth]
        else:
            arrived(has_next, back_low, retlow_dst)
            remainder[l] += dot_nt(retlow_dst[...], pick[l])
            arrived(has_next, back_second, ret2_dst)
            left = ret2_dst[...]
        remainder[l] = jnp.where(masks[l], remainder[l], 0.0)
        second[l] = jnp.where(masks[l], right + gather(l, left), 0.0)

    outer = unpack(collect(len(stages) - 1, trailing[-1], last_src, last_dst), loads)
    outer = 0.5 * (outer + outer.T)
    again = small_tn(alpha, small(outer, alpha) - known)
    alpha2 = eliminate(again, right_side)
    for l in range(number):
        following = small_tn(shift, search[l]) - small_tn(alpha, scaled[l])
        solution_ref[l] = small_tn(alpha, search[l]) + small_tn(alpha2, following)
        moved = small_tn(shift, image[l] + remainder[l]) - small_tn(alpha, second[l])
        residual_ref[l] = start[l] - small_tn(alpha, image[l]) - small_tn(alpha2, moved)

    @pl.when(has_next)
    def _():
        for copy in (forward, forward_low, forward_second):
            copy.wait_send()

    @pl.when(has_prev)
    def _():
        for copy in (back, back_low, back_second):
            copy.wait_send()

    for copies in pending + trailing:
        for copy in copies:
            copy.wait_send()


def body(stages, devs, total, operators, forces, weights, lengths, slot_order):
    number, loads, breadth = forces.shape
    tall, wide = jax.eval_shape(pack, jax.ShapeDtypeStruct((loads, loads), F32)).shape
    boxes = sum(stage[0] - 1 for stage in stages)
    field = pltpu.VMEM(forces.shape, F32)
    vmem = pl.BlockSpec(memory_space=pltpu.VMEM)
    return tuple(pl.pallas_call(
        functools.partial(kernel, stages, devs, total),
        out_shape=[jax.ShapeDtypeStruct(forces.shape, F32)] * 2,
        in_specs=[pl.BlockSpec(memory_space=pl.ANY)] * 5,
        out_specs=[vmem, vmem],
        scratch_shapes=[
            pltpu.SMEM(lengths.shape, jnp.int32),
            field,
            pltpu.VMEM(weights.shape, F32),
            pltpu.VMEM(slot_order.shape, jnp.int32),
            pltpu.VMEM(operators.shape, BF16),
            pltpu.VMEM((number, breadth, breadth), BF16),
            field, field, field, field, field, field,
            pltpu.VMEM((number, 2 * loads, 2 * breadth), F32),
            pltpu.VMEM((2, loads, breadth), BF16),
            pltpu.VMEM((2, loads, breadth), BF16),
            pltpu.VMEM((2 * loads, breadth), BF16),
            pltpu.VMEM((2 * loads, breadth), BF16),
            pltpu.VMEM((loads, breadth), F32),
            pltpu.VMEM((loads, breadth), F32),
            pltpu.VMEM((loads, breadth), BF16),
            pltpu.VMEM((loads, breadth), BF16),
            pltpu.VMEM((loads, breadth), F32),
            pltpu.VMEM((loads, breadth), F32),
            pltpu.VMEM((len(stages), 3 * tall, wide), F32),
            pltpu.VMEM((boxes, 3 * tall, wide), F32),
            pltpu.VMEM((len(stages), tall, wide), F32),
            pltpu.VMEM((boxes, tall, wide), F32),
            pltpu.SemaphoreType.DMA((number,)),
            pltpu.SemaphoreType.DMA((4,)),
            pltpu.SemaphoreType.DMA((6,)),
            pltpu.SemaphoreType.DMA((6,)),
            pltpu.SemaphoreType.DMA((boxes,)),
            pltpu.SemaphoreType.DMA((boxes,)),
            pltpu.SemaphoreType.DMA((boxes,)),
            pltpu.SemaphoreType.DMA((boxes,)),
        ],
        compiler_params=pltpu.CompilerParams(
            collective_id=0, has_side_effects=True, vmem_limit_bytes=60 * 1024 * 1024
        ),
        cost_estimate=pl.CostEstimate(
            flops=12 * number * loads * 4 * breadth * breadth,
            bytes_accessed=operators.size * 2 + 4 * forces.size * 4,
            transcendentals=0,
        ),
    )(lengths, forces, weights, slot_order, operators))


def solution(mesh):
    devs, groups = mesh.shape["dev"], mesh.shape["grp"]
    stages = plan_stages(groups, devs)
    in_specs = (
        P(("grp", "dev"), None, None),
        P(("grp", "dev"), None, None),
        P(("grp", "dev"), None),
        P(),
        P(("grp", "dev"), None),
    )
    out_specs = (P(("grp", "dev"), None, None), P(("grp", "dev"), None, None))
    return jax.shard_map(
        functools.partial(body, stages, devs, devs * groups),
        mesh=mesh, in_specs=in_specs, out_specs=out_specs, check_vma=False,
    )
```

profile of v0, /device:TPU:0, one launch (start us, length us, event | category | flops | bytes accessed | tf_op | source)
XLA Modules:
  0.0 34.1 jit_solution(14164622405837623240)
XLA Ops:
  0.6 30.3 %shard_map.68 = (f32[2,32,512]{2,1,0:T(8,128)}, f32[2,32,512]{2,1,0:T(8,128)}) custom-call(s32[64]{0:T(128)} %lengths_hbm.1, f32[2,32,512]{2,1,0:T(8,128)} %forces_hbm.1, f32[2,512]{1,0:T(2,128)} %weights_hbm.1, s32[2,512]{1,0:T(2,128)} %order_hbm.1, bf16[2,1024,1024]{2,1,0:T(8,128)(2,1)} %operators_ref.1), custom_call_target="tpu_custom_call" | custom-call | flops 805306368 | bytes 4718592 | tf_op jit(solution)/shard_map/pallas_call | solution.py:358
  31.0 1.6 %copy.9 = f32[2,32,512]{2,1,0:T(8,128)} copy(f32[2,32,512]{2,1,0:T(8,128)} %get-tuple-element.4) | data formatting | bytes 262144
  32.5 1.6 %copy.10 = f32[2,32,512]{2,1,0:T(8,128)} copy(f32[2,32,512]{2,1,0:T(8,128)} %get-tuple-element.5) | data formatting | bytes 262144
where the time goes:
time: 34.3 us; the launch traced here: 34.1 us
  Pallas kernels  30.3 us (88%)
  local copies, waits for them, and re-layouts  3.14 us (9%)
  between operations  0.64 us (2%)
    pallas_call x1, Pallas kernels, body(): pl.pallas_call(functools.partial(kernel, stages, devs, total), out_shape=...  30.3 us
    unnamed x2, local copies, waits for them, and re-layouts  3.14 us

commit v1 on v0

--- a/solution.py
+++ b/solution.py
@@ -9,6 +9,7 @@
 
 MESH = pl.DeviceIdType.MESH
 F32, BF16 = jnp.float32, jnp.bfloat16
+VMEM_BYTES = 60 * 1024 * 1024
 EXACT = lax.Precision.HIGHEST
 
 
@@ -107,8 +108,8 @@
 
 def kernel(stages, devs, total, lengths_hbm, forces_hbm, weights_hbm, order_hbm, operators_ref,
            solution_ref, residual_ref,
-           lengths_ref, forces_ref, weights_ref, order_ref, ops, pick, start, search, image, remainder, scaled, second, product,
-           fwd_src, fwd_dst, fwd2_src, fwd2_dst, ret_src, ret_dst, retlow_src, retlow_dst,
+           lengths_ref, forces_ref, weights_ref, order_ref, ops, pick, start, search, image, remainder, scaled, second, product, applied,
+           fwd_src, fwd_dst, fwdlow_src, fwdlow_dst, right_src, right_dst, ret_src, ret_dst, retlow_src, retlow_dst,
            ret2_src, ret2_dst, sums_src, sums_dst, last_src, last_dst,
            ops_sem, small_sem, halo_send, halo_recv, sums_send, sums_recv, last_send, last_recv):
     number, loads, breadth = forces_ref.shape
@@ -142,7 +143,7 @@
     ]
     for copy in fetching:
         copy.start()
-    loading = [pltpu.make_async_copy(operators_ref.at[l], ops.at[l], ops_sem.at[l]) for l in range(number)]
+    loading = [pltpu.make_async_copy(operators_ref.at[l], ops.at[l], ops_sem.at[l]) for l in reversed(range(number))]
     for copy in loading:
         copy.start()
 
@@ -152,9 +153,9 @@
             device_id=where, device_id_type=MESH,
         )
 
-    forward = remote(0, fwd_src.at[0], fwd_dst.at[0], next_id)
-    forward_low = remote(1, fwd_src.at[1], fwd_dst.at[1], next_id)
-    forward_second = remote(2, fwd2_src, fwd2_dst, next_id)
+    forward = remote(0, fwd_src, fwd_dst, next_id)
+    forward_low = remote(1, fwdlow_src, fwdlow_dst, next_id)
+    forward_right = remote(2, right_src, right_dst, next_id)
     back = remote(3, ret_src, ret_dst, prev_id)
     back_low = remote(4, retlow_src, retlow_dst, prev_id)
     back_second = remote(5, ret2_src, ret2_dst, prev_id)
@@ -184,70 +185,79 @@
         masks.append(positions < live)
     slots = lax.broadcasted_iota(jnp.int32, (breadth, breadth), 0)
 
+    last = number - 1
     turned = [None] * number
     stacks = [None] * number
     for l in reversed(range(number)):
         pick[l] = jnp.where(slots == order_ref[l : l + 1, :], 1.0, 0.0).astype(BF16)
         start[l] = jnp.where(masks[l], forces_ref[l], 0.0)
         search[l] = start[l] * weights_ref[l : l + 1, :]
-        high, low = split(search[l])
-        stacks[l] = jnp.concatenate([high, low], axis=0)
-        turned[l] = dot(stacks[l], pick[l]).astype(BF16)
-        if l == number - 1:
-            fwd_src[0] = turned[l][:loads]
-            fwd_src[1] = turned[l][loads:]
+        stacks[l] = jnp.concatenate(split(search[l]), axis=0)
+        if l == last:
+            spread = [jnp.broadcast_to(x, (16, breadth)) for x in split(weights_ref[l : l + 1, :])]
+            sent = dot(jnp.concatenate([stacks[l]] + spread, axis=0), pick[l]).astype(BF16)
+            fwd_src[...] = sent[:loads]
+            fwdlow_src[...] = sent[loads:]
             pl.semaphore_wait(barrier, partners + has_prev.astype(jnp.int32) + has_next.astype(jnp.int32))
             start_if(has_next, forward, forward_low)
-
-    for copy in loading:
+        else:
+            turned[l] = dot(stacks[l], pick[l]).astype(BF16)
+
+    def gather(l, field):
+        both = dot_nt(jnp.concatenate(split(field), axis=0), pick[l])
+        return both[:loads] + both[loads:]
+
+    def apply(l, fields, target):
+        target[l] = dot(jnp.concatenate(fields, axis=1), ops[l])
+
+    loading[0].wait()
+    apply(last, [turned[last - 1], stacks[last]], product)
+    both = dot(jnp.concatenate(split(product[last, :loads, breadth:]), axis=0), pick[last])
+    right_src[...] = both[:loads] + both[loads:]
+    start_if(has_next, forward_right)
+    for copy in loading[1:]:
         copy.wait()
-
-    def own_products(stacks, turned):
-        product[0] = dot(stacks[0], ops[0, breadth:, :])
-        for l in range(1, number):
-            product[l] = dot(jnp.concatenate([turned[l - 1], stacks[l]], axis=1), ops[l])
-
-    def gather(l, field):
-        high, low = split(field)
-        both = dot_nt(jnp.concatenate([high, low], axis=0), pick[l])
-        return both[:loads] + both[loads:]
-
-    own_products(stacks, turned)
-    arrived(has_prev, forward, fwd_dst.at[0])
-    ret_src[...] = product[0, :loads, :breadth] + dot(fwd_dst[0], ops[0, :breadth, :breadth])
-    start_if(has_prev, back)
-    product[0, :loads, breadth:] += dot(fwd_dst[0], ops[0, :breadth, breadth:])
-    arrived(has_prev, forward_low, fwd_dst.at[1])
-    product[0, loads:, :] += dot(fwd_dst[1], ops[0, :breadth, :])
-    retlow_src[...] = product[0, loads:, :breadth].astype(BF16)
-    start_if(has_prev, back_low)
+    for l in range(1, last):
+        apply(l, [turned[l - 1], stacks[l]], product)
+    product[0] = dot(stacks[0], ops[0, breadth:, :])
+    projection = 0.0
+    for l in range(number):
+        projection = projection + dot_nt(search[l], start[l], EXACT)
 
     def finish_image(l, left):
         image[l] = jnp.where(masks[l], product[l, :loads, breadth:] + gather(l, left), 0.0)
         scaled[l] = weights_ref[l : l + 1, :] * image[l]
-        high, low = split(scaled[l])
-        stacks[l] = jnp.concatenate([high, low], axis=0)
+        stacks[l] = jnp.concatenate(split(scaled[l]), axis=0)
+
+    def gram(direction, along, values):
+        pair = dot_nt(jnp.concatenate([direction, along], axis=0), values, EXACT)
+        return pair[:loads], pair[loads:]
+
+    arrived(has_prev, forward, fwd_dst)
+    owed = product[0, :loads, :breadth] + dot(fwd_dst[...], ops[0, :breadth, :breadth])
+    ret_src[...] = owed
+    start_if(has_prev, back)
+    product[0, :loads, breadth:] += dot(fwd_dst[...], ops[0, :breadth, breadth:])
+    curvature = middle = 0.0
+    for l in range(last):
+        finish_image(l, product[l + 1, :loads, :breadth])
         turned[l] = dot(stacks[l], pick[l]).astype(BF16)
-
-    def gram(l):
-        pair = dot_nt(jnp.concatenate([search[l], scaled[l]], axis=0), image[l], EXACT)
-        return pair[:loads], pair[loads:]
-
-    curvature = projection = middle = 0.0
-    for l in range(number):
-        remainder[l] = product[l, loads:, breadth:]
-        projection = projection + dot_nt(search[l], start[l], EXACT)
-        if l < number - 1:
-            finish_image(l, product[l + 1, :loads, :breadth])
-            remainder[l] += dot_nt(product[l + 1, loads:, :breadth].astype(BF16), pick[l])
-            first, second_part = gram(l)
-            curvature, middle = curvature + first, middle + second_part
-    arrived(has_next, back, ret_dst)
-    finish_image(number - 1, ret_dst[...])
-    fwd2_src[...] = turned[number - 1]
-    start_if(has_next, forward_second)
-    first, second_part = gram(number - 1)
-    curvature, middle = curvature + first, middle + second_part
+        first, other = gram(search[l], scaled[l], image[l])
+        curvature, middle = curvature + first, middle + other
+
+    arrived(has_prev, forward_low, fwdlow_dst)
+    arrived(has_prev, forward_right, right_dst)
+    incoming = positions < jnp.where(has_prev, lengths_ref[jnp.maximum(me * number - 1, 0)], 0)
+    across = jnp.where(incoming, right_dst[...] + owed, 0.0)
+    turned_weights = (
+        fwdlow_dst[loads : loads + 16].astype(F32) + fwdlow_dst[loads + 16 : loads + 32].astype(F32)
+    )[:1]
+    across_scaled = turned_weights * across
+    across_stack = jnp.concatenate(split(across_scaled), axis=0)
+    first, other = gram(
+        fwd_dst[...].astype(F32) + fwdlow_dst[:loads].astype(F32), across_scaled, across
+    )
+    curvature, middle = curvature + first, middle + other
 
     def exchange(s, source, inbox, send_sem, recv_sem):
         copies = []
@@ -273,30 +283,35 @@
     sums_src[0] = jnp.concatenate([pack(curvature), pack(projection), pack(middle)], axis=0)
     pending = [exchange(0, sums_src, sums_dst, sums_send, sums_recv)]
 
-    own_products(stacks, turned)
-
     def energy(pair, values):
         return dot_nt(pair[:loads].astype(F32) + pair[loads:].astype(F32), values[:loads] + values[loads:], EXACT)
 
-    outer = 0.0
-    for l in range(number):
-        outer = outer + energy(stacks[l], product[l, :, breadth:])
-        if l > 0:
-            outer = outer + energy(turned[l - 1], product[l, :, :breadth])
+    apply(0, [across_stack, stacks[0]], applied)
+    ret2_src[...] = applied[0, :loads, :breadth] + applied[0, loads:, :breadth]
+    outer = energy(across_stack, applied[0, :, :breadth]) + energy(stacks[0], applied[0, :, breadth:])
+    for l in range(1, last):
+        apply(l, [turned[l - 1], stacks[l]], applied)
+        outer = outer + energy(turned[l - 1], applied[l, :, :breadth]) + energy(stacks[l], applied[l, :, breadth:])
+    applied[last] = dot(turned[last - 1], ops[last, :breadth, :])
+    outer = outer + energy(turned[last - 1], applied[last, :, :breadth])
+
     for s in range(1, len(stages)):
         sums_src[s] = collect(s - 1, pending[-1], sums_src, sums_dst)
         pending.append(exchange(s, sums_src, sums_dst, sums_send, sums_recv))
-    arrived(has_prev, forward_second, fwd2_dst)
-    left_own = product[0, :, :breadth]
-    left_extra = dot(fwd2_dst[...], ops[0, :breadth, :breadth])
-    mixed = energy(fwd2_dst[...], left_extra + 2.0 * left_own)
-    outer = outer + mixed
+
+    arrived(has_next, back, ret_dst)
+    finish_image(last, ret_dst[...])
+    own = dot(stacks[last], ops[last, breadth:, breadth:])
+    outer = outer + energy(stacks[last], own + 2.0 * applied[last, :, breadth:])
     last_src[0] = pack(outer)
     trailing = [exchange(0, last_src, last_dst, last_send, last_recv)]
-    left_total = left_own + left_extra
-    ret2_src[...] = left_total[:loads] + left_total[loads:]
     start_if(has_prev, back_second)
-    product[0, :, breadth:] += dot(fwd2_dst[...], ops[0, :breadth, breadth:])
+
+    product[0, loads:, :] += dot(fwdlow_dst[:loads], ops[0, :breadth, :])
+    retlow_src[...] = product[0, loads:, :breadth].astype(BF16)
+    start_if(has_prev, back_low)
+    applied[last, :, breadth:] += own
+    applied[last, :, :breadth] += dot(stacks[last], ops[last, breadth:, :breadth])
 
     def advance():
         for s in range(1, len(stages)):
@@ -313,17 +328,17 @@
     right_side = small_tn(alpha, small(middle, alpha) - curvature)
     known = small(middle, shift)
     for l in range(number):
-        right = product[l, :loads, breadth:] + product[l, loads:, breadth:]
-        if l < number - 1:
-            left = product[l + 1, :loads, :breadth] + product[l + 1, loads:, :breadth]
+        right = applied[l, :loads, breadth:] + applied[l, loads:, breadth:]
+        if l < last:
+            left_low = product[l + 1, loads:, :breadth].astype(BF16)
+            left = applied[l + 1, :loads, :breadth] + applied[l + 1, loads:, :breadth]
         else:
             arrived(has_next, back_low, retlow_dst)
-            remainder[l] += dot_nt(retlow_dst[...], pick[l])
+            left_low = retlow_dst[...]
             arrived(has_next, back_second, ret2_dst)
             left = ret2_dst[...]
-        remainder[l] = jnp.where(masks[l], remainder[l], 0.0)
+        remainder[l] = jnp.where(masks[l], product[l, loads:, breadth:] + dot_nt(left_low, pick[l]), 0.0)
         second[l] = jnp.where(masks[l], right + gather(l, left), 0.0)
-
     outer = unpack(collect(len(stages) - 1, trailing[-1], last_src, last_dst), loads)
     outer = 0.5 * (outer + outer.T)
     again = small_tn(alpha, small(outer, alpha) - known)
@@ -336,7 +351,7 @@
 
     @pl.when(has_next)
     def _():
-        for copy in (forward, forward_low, forward_second):
+        for copy in (forward, forward_low, forward_right):
             copy.wait_send()
 
     @pl.when(has_prev)
@@ -347,6 +362,31 @@
     for copies in pending + trailing:
         for copy in copies:
             copy.wait_send()
+
+
+def hand_over(*fields):
+    count, number = len(fields), fields[0].shape[0]
+
+    def copies(*refs):
+        sources, targets, sems = refs[:count], refs[count : 2 * count], refs[2 * count]
+        moving = [
+            pltpu.make_async_copy(sources[i].at[l], targets[i].at[l], sems.at[i * number + l])
+            for i in range(count) for l in range(number)
+        ]
+        for copy in moving:
+            copy.start()
+        for copy in moving:
+            copy.wait()
+
+    anywhere = pl.BlockSpec(memory_space=pl.ANY)
+    return tuple(pl.pallas_call(
+        copies,
+        out_shape=[jax.ShapeDtypeStruct(field.shape, field.dtype) for field in fields],
+        in_specs=[anywhere] * count,
+        out_specs=[anywhere] * count,
+        scratch_shapes=[pltpu.SemaphoreType.DMA((count * number,))],
+        compiler_params=pltpu.CompilerParams(vmem_limit_bytes=VMEM_BYTES),
+    )(*fields))
 
 
 def body(stages, devs, total, operators, forces, weights, lengths, slot_order):
@@ -355,7 +395,7 @@
     boxes = sum(stage[0] - 1 for stage in stages)
     field = pltpu.VMEM(forces.shape, F32)
     vmem = pl.BlockSpec(memory_space=pltpu.VMEM)
-    return tuple(pl.pallas_call(
+    results = pl.pallas_call(
         functools.partial(kernel, stages, devs, total),
         out_shape=[jax.ShapeDtypeStruct(forces.shape, F32)] * 2,
         in_specs=[pl.BlockSpec(memory_space=pl.ANY)] * 5,
@@ -369,10 +409,13 @@
             pltpu.VMEM((number, breadth, breadth), BF16),
             field, field, field, field, field, field,
             pltpu.VMEM((number, 2 * loads, 2 * breadth), F32),
-            pltpu.VMEM((2, loads, breadth), BF16),
-            pltpu.VMEM((2, loads, breadth), BF16),
-            pltpu.VMEM((2 * loads, breadth), BF16),
-            pltpu.VMEM((2 * loads, breadth), BF16),
+            pltpu.VMEM((number, 2 * loads, 2 * breadth), F32),
+            pltpu.VMEM((loads, breadth), BF16),
+            pltpu.VMEM((loads, breadth), BF16),
+            pltpu.VMEM((loads + 32, breadth), BF16),
+            pltpu.VMEM((loads + 32, breadth), BF16),
+            pltpu.VMEM((loads, breadth), F32),
+            pltpu.VMEM((loads, breadth), F32),
             pltpu.VMEM((loads, breadth), F32),
             pltpu.VMEM((loads, breadth), F32),
             pltpu.VMEM((loads, breadth), BF16),
@@ -393,14 +436,15 @@
             pltpu.SemaphoreType.DMA((boxes,)),
         ],
         compiler_params=pltpu.CompilerParams(
-            collective_id=0, has_side_effects=True, vmem_limit_bytes=60 * 1024 * 1024
+            collective_id=0, has_side_effects=True, vmem_limit_bytes=VMEM_BYTES
         ),
         cost_estimate=pl.CostEstimate(
             flops=12 * number * loads * 4 * breadth * breadth,
             bytes_accessed=operators.size * 2 + 4 * forces.size * 4,
             transcendentals=0,
         ),
-    )(lengths, forces, weights, slot_order, operators))
+    )(lengths, forces, weights, slot_order, operators)
+    return hand_over(*results)
 
 
 def solution(mesh):

time: 34.3 us -> 37.6 us (1.096)
  Pallas kernels: 30.3 us -> 36.8 us
  local copies, waits for them, and re-layouts: 3.14 us -> 0 us
    pallas_call x0 -> x1, Pallas kernels: none -> 9.08 us  [hand_over(): pl.pallas_call(copies, out_shape=[jax.ShapeDtypeStruct(field.shape, field...]
    unnamed x2 -> x0, local copies, waits for them, and re-layouts: 3.14 us -> none
    pallas_call x1, Pallas kernels: 30.3 us -> 27.7 us  [body(): pl.pallas_call(functools.partial(kernel, stages, devs, total), out_shape=...]
where the time goes in v1:
time: 37.6 us; the launch traced here: 37.4 us
  Pallas kernels  36.8 us (98%)
  between operations  0.64 us (2%)
    pallas_call x1, Pallas kernels, body(): pl.pallas_call(functools.partial(kernel, stages, devs, total), out_shape=...  27.7 us
    pallas_call x1, Pallas kernels, hand_over(): pl.pallas_call(copies, out_shape=[jax.ShapeDtypeStruct(field.shape, field...  9.08 us

profile of v1, /device:TPU:0, one launch (start us, length us, event | category | flops | bytes accessed | tf_op | source)
XLA Modules:
  0.0 37.4 jit_solution(3759256608342087515)
XLA Ops:
  0.6 27.7 %shard_map.68 = (f32[2,32,512]{2,1,0:T(8,128)}, f32[2,32,512]{2,1,0:T(8,128)}) custom-call(s32[64]{0:T(128)} %lengths_hbm.1, f32[2,32,512]{2,1,0:T(8,128)} %forces_hbm.1, f32[2,512]{1,0:T(2,128)} %weights_hbm.1, s32[2,512]{1,0:T(2,128)} %order_hbm.1, bf16[2,1024,1024]{2,1,0:T(8,128)(2,1)} %operators_ref.1), custom_call_target="tpu_custom_call" | custom-call | flops 805306368 | bytes 4718592 | tf_op jit(solution)/shard_map/pallas_call | solution.py:398
  28.3 9.1 %shard_map.69 = (f32[2,32,512]{2,1,0:T(8,128)}, f32[2,32,512]{2,1,0:T(8,128)}) custom-call(f32[2,32,512]{2,1,0:T(8,128)} %get-tuple-element.4.refs_0_, f32[2,32,512]{2,1,0:T(8,128)} %get-tuple-element.5.refs_1_), custom_call_target="tpu_custom_call" | custom-call | tf_op jit(solution)/shard_map/pallas_call | solution.py:382

commit v2 on v1

--- a/solution.py
+++ b/solution.py
@@ -108,7 +108,7 @@
 
 def kernel(stages, devs, total, lengths_hbm, forces_hbm, weights_hbm, order_hbm, operators_ref,
            solution_ref, residual_ref,
-           lengths_ref, forces_ref, weights_ref, order_ref, ops, pick, start, search, image, remainder, scaled, second, product, applied,
+           lengths_ref, forces_ref, weights_ref, order_ref, ops, pick, start, search, image, remainder, scaled, second, following, product, applied,
            fwd_src, fwd_dst, fwdlow_src, fwdlow_dst, right_src, right_dst, ret_src, ret_dst, retlow_src, retlow_dst,
            ret2_src, ret2_dst, sums_src, sums_dst, last_src, last_dst,
            ops_sem, small_sem, halo_send, halo_recv, sums_send, sums_recv, last_send, last_recv):
@@ -211,53 +211,31 @@
         target[l] = dot(jnp.concatenate(fields, axis=1), ops[l])
 
     loading[0].wait()
-    apply(last, [turned[last - 1], stacks[last]], product)
+    joined = jnp.concatenate([turned[last - 1], stacks[last]], axis=1)
+    product[last, :, breadth:] = dot(joined, ops[last, :, breadth:])
     both = dot(jnp.concatenate(split(product[last, :loads, breadth:]), axis=0), pick[last])
     right_src[...] = both[:loads] + both[loads:]
     start_if(has_next, forward_right)
+    product[last, :, :breadth] = dot(joined, ops[last, :, :breadth])
     for copy in loading[1:]:
         copy.wait()
     for l in range(1, last):
         apply(l, [turned[l - 1], stacks[l]], product)
     product[0] = dot(stacks[0], ops[0, breadth:, :])
-    projection = 0.0
+    def whole(pair):
+        return pair[:loads].astype(F32) + pair[loads:].astype(F32)
+
+    projection = curvature = 0.0
     for l in range(number):
         projection = projection + dot_nt(search[l], start[l], EXACT)
+        if l > 0:
+            curvature = curvature + dot_nt(search[l], product[l, :loads, breadth:], EXACT)
+            curvature = curvature + dot_nt(whole(turned[l - 1]), product[l, :loads, :breadth], EXACT)
 
     def finish_image(l, left):
         image[l] = jnp.where(masks[l], product[l, :loads, breadth:] + gather(l, left), 0.0)
         scaled[l] = weights_ref[l : l + 1, :] * image[l]
         stacks[l] = jnp.concatenate(split(scaled[l]), axis=0)
-
-    def gram(direction, along, values):
-        pair = dot_nt(jnp.concatenate([direction, along], axis=0), values, EXACT)
-        return pair[:loads], pair[loads:]
-
-    arrived(has_prev, forward, fwd_dst)
-    owed = product[0, :loads, :breadth] + dot(fwd_dst[...], ops[0, :breadth, :breadth])
-    ret_src[...] = owed
-    start_if(has_prev, back)
-    product[0, :loads, breadth:] += dot(fwd_dst[...], ops[0, :breadth, breadth:])
-    curvature = middle = 0.0
-    for l in range(last):
-        finish_image(l, product[l + 1, :loads, :breadth])
-        turned[l] = dot(stacks[l], pick[l]).astype(BF16)
-        first, other = gram(search[l], scaled[l], image[l])
-        curvature, middle = curvature + first, middle + other
-
-    arrived(has_prev, forward_low, fwdlow_dst)
-    arrived(has_prev, forward_right, right_dst)
-    incoming = positions < jnp.where(has_prev, lengths_ref[jnp.maximum(me * number - 1, 0)], 0)
-    across = jnp.where(incoming, right_dst[...] + owed, 0.0)
-    turned_weights = (
-        fwdlow_dst[loads : loads + 16].astype(F32) + fwdlow_dst[loads + 16 : loads + 32].astype(F32)
-    )[:1]
-    across_scaled = turned_weights * across
-    across_stack = jnp.concatenate(split(across_scaled), axis=0)
-    first, other = gram(
-        fwd_dst[...].astype(F32) + fwdlow_dst[:loads].astype(F32), across_scaled, across
-    )
-    curvature, middle = curvature + first, middle + other
 
     def exchange(s, source, inbox, send_sem, recv_sem):
         copies = []
@@ -279,12 +257,38 @@
             value = value + inbox[first + i]
         return value
 
+    arrived(has_prev, forward, fwd_dst)
+    owed = product[0, :loads, :breadth] + dot(fwd_dst[...], ops[0, :breadth, :breadth])
+    ret_src[...] = owed
+    start_if(has_prev, back)
+    product[0, :loads, breadth:] += dot(fwd_dst[...], ops[0, :breadth, breadth:])
+    arrived(has_prev, forward_low, fwdlow_dst)
+    curvature = curvature + dot_nt(search[0], product[0, :loads, breadth:], EXACT)
+    curvature = curvature + dot_nt(
+        fwd_dst[...].astype(F32) + fwdlow_dst[:loads].astype(F32), owed, EXACT
+    )
     tall = pack(curvature).shape[0]
-    sums_src[0] = jnp.concatenate([pack(curvature), pack(projection), pack(middle)], axis=0)
+    sums_src[0] = jnp.concatenate([pack(curvature), pack(projection)], axis=0)
     pending = [exchange(0, sums_src, sums_dst, sums_send, sums_recv)]
 
+    middle = 0.0
+    for l in range(last):
+        finish_image(l, product[l + 1, :loads, :breadth])
+        turned[l] = dot(stacks[l], pick[l]).astype(BF16)
+        middle = middle + dot_nt(scaled[l], image[l], EXACT)
+
+    arrived(has_prev, forward_right, right_dst)
+    incoming = positions < jnp.where(has_prev, lengths_ref[jnp.maximum(me * number - 1, 0)], 0)
+    across = jnp.where(incoming, right_dst[...] + owed, 0.0)
+    turned_weights = (
+        fwdlow_dst[loads : loads + 16].astype(F32) + fwdlow_dst[loads + 16 : loads + 32].astype(F32)
+    )[:1]
+    across_scaled = turned_weights * across
+    across_stack = jnp.concatenate(split(across_scaled), axis=0)
+    middle = middle + dot_nt(across_scaled, across, EXACT)
+
     def energy(pair, values):
-        return dot_nt(pair[:loads].astype(F32) + pair[loads:].astype(F32), values[:loads] + values[loads:], EXACT)
+        return dot_nt(whole(pair), values[:loads] + values[loads:], EXACT)
 
     apply(0, [across_stack, stacks[0]], applied)
     ret2_src[...] = applied[0, :loads, :breadth] + applied[0, loads:, :breadth]
@@ -303,7 +307,7 @@
     finish_image(last, ret_dst[...])
     own = dot(stacks[last], ops[last, breadth:, breadth:])
     outer = outer + energy(stacks[last], own + 2.0 * applied[last, :, breadth:])
-    last_src[0] = pack(outer)
+    last_src[0] = jnp.concatenate([pack(middle), pack(outer)], axis=0)
     trailing = [exchange(0, last_src, last_dst, last_send, last_recv)]
     start_if(has_prev, back_second)
 
@@ -320,13 +324,12 @@
 
     summed = collect(len(stages) - 1, pending[-1], sums_src, sums_dst)
     curvature = unpack(summed[:tall], loads)
-    projection = unpack(summed[tall : 2 * tall], loads)
-    middle = unpack(summed[2 * tall :], loads)
-    solved = eliminate(curvature, jnp.concatenate([projection, middle], axis=1), advance)
-    alpha = solved[:, :loads]
-    shift = small(solved[:, loads:], alpha)
-    right_side = small_tn(alpha, small(middle, alpha) - curvature)
-    known = small(middle, shift)
+    projection = unpack(summed[tall:], loads)
+    identity = jnp.where(
+        lax.broadcasted_iota(jnp.int32, (loads, loads), 0) == lax.broadcasted_iota(jnp.int32, (loads, loads), 1), 1.0, 0.0
+    )
+    solved = eliminate(curvature, jnp.concatenate([projection, identity], axis=1), advance)
+    alpha, inverse = solved[:, :loads], solved[:, loads:]
     for l in range(number):
         right = applied[l, :loads, breadth:] + applied[l, loads:, breadth:]
         if l < last:
@@ -339,15 +342,22 @@
             left = ret2_dst[...]
         remainder[l] = jnp.where(masks[l], product[l, loads:, breadth:] + dot_nt(left_low, pick[l]), 0.0)
         second[l] = jnp.where(masks[l], right + gather(l, left), 0.0)
-    outer = unpack(collect(len(stages) - 1, trailing[-1], last_src, last_dst), loads)
+    for l in range(number):
+        solution_ref[l] = small_tn(alpha, search[l])
+        residual_ref[l] = start[l] - small_tn(alpha, image[l])
+        following[l] = small_tn(alpha, scaled[l])
+        second[l] = small_tn(alpha, second[l])
+        image[l] += remainder[l]
+    summed = collect(len(stages) - 1, trailing[-1], last_src, last_dst)
+    middle, outer = unpack(summed[:tall], loads), unpack(summed[tall:], loads)
     outer = 0.5 * (outer + outer.T)
-    again = small_tn(alpha, small(outer, alpha) - known)
-    alpha2 = eliminate(again, right_side)
+    carried = small(middle, alpha)
+    shift = small(inverse, carried)
+    again = small_tn(alpha, small(outer, alpha) - small(middle, shift))
+    alpha2 = eliminate(again, small_tn(alpha, carried - curvature))
     for l in range(number):
-        following = small_tn(shift, search[l]) - small_tn(alpha, scaled[l])
-        solution_ref[l] = small_tn(alpha, search[l]) + small_tn(alpha2, following)
-        moved = small_tn(shift, image[l] + remainder[l]) - small_tn(alpha, second[l])
-        residual_ref[l] = start[l] - small_tn(alpha, image[l]) - small_tn(alpha2, moved)
+        solution_ref[l] += small_tn(alpha2, small_tn(shift, search[l]) - following[l])
+        residual_ref[l] -= small_tn(alpha2, small_tn(shift, image[l]) - second[l])
 
     @pl.when(has_next)
     def _():
@@ -368,14 +378,21 @@
     count, number = len(fields), fields[0].shape[0]
 
     def copies(*refs):
-        sources, targets, sems = refs[:count], refs[count : 2 * count], refs[2 * count]
-        moving = [
-            pltpu.make_async_copy(sources[i].at[l], targets[i].at[l], sems.at[i * number + l])
-            for i in range(count) for l in range(number)
+        sources, targets = refs[:count], refs[count : 2 * count]
+        held, in_sems, out_sems = refs[2 * count :]
+        places = [(i, l) for i in range(count) for l in range(number)]
+        inward = [
+            pltpu.make_async_copy(sources[i].at[l], held.at[n], in_sems.at[n]) for n, (i, l) in enumerate(places)
         ]
-        for copy in moving:
+        outward = [
+            pltpu.make_async_copy(held.at[n], targets[i].at[l], out_sems.at[n]) for n, (i, l) in enumerate(places)
+        ]
+        for copy in inward:
             copy.start()
-        for copy in moving:
+        for arriving, leaving in zip(inward, outward):
+            arriving.wait()
+            leaving.start()
+        for copy in outward:
             copy.wait()
 
     anywhere = pl.BlockSpec(memory_space=pl.ANY)
@@ -384,7 +401,11 @@
         out_shape=[jax.ShapeDtypeStruct(field.shape, field.dtype) for field in fields],
         in_specs=[anywhere] * count,
         out_specs=[anywhere] * count,
-        scratch_shapes=[pltpu.SemaphoreType.DMA((count * number,))],
+        scratch_shapes=[
+            pltpu.VMEM((count * number,) + fields[0].shape[1:], fields[0].dtype),
+            pltpu.SemaphoreType.DMA((count * number,)),
+            pltpu.SemaphoreType.DMA((count * number,)),
+        ],
         compiler_params=pltpu.CompilerParams(vmem_limit_bytes=VMEM_BYTES),
     )(*fields))
 
@@ -407,7 +428,7 @@
             pltpu.VMEM(slot_order.shape, jnp.int32),
             pltpu.VMEM(operators.shape, BF16),
             pltpu.VMEM((number, breadth, breadth), BF16),
-            field, field, field, field, field, field,
+            field, field, field, field, field, field, field,
             pltpu.VMEM((number, 2 * loads, 2 * breadth), F32),
             pltpu.VMEM((number, 2 * loads, 2 * breadth), F32),
             pltpu.VMEM((loads, breadth), BF16),
@@ -422,10 +443,10 @@
             pltpu.VMEM((loads, breadth), BF16),
             pltpu.VMEM((loads, breadth), F32),
             pltpu.VMEM((loads, breadth), F32),
-            pltpu.VMEM((len(stages), 3 * tall, wide), F32),
-            pltpu.VMEM((boxes, 3 * tall, wide), F32),
-            pltpu.VMEM((len(stages), tall, wide), F32),
-            pltpu.VMEM((boxes, tall, wide), F32),
+            pltpu.VMEM((len(stages), 2 * tall, wide), F32),
+            pltpu.VMEM((boxes, 2 * tall, wide), F32),
+            pltpu.VMEM((len(stages), 2 * tall, wide), F32),
+            pltpu.VMEM((boxes, 2 * tall, wide), F32),
             pltpu.SemaphoreType.DMA((number,)),
             pltpu.SemaphoreType.DMA((4,)),
             pltpu.SemaphoreType.DMA((6,)),

time: 37.6 us -> 28.5 us (0.76)
  Pallas kernels: 36.8 us -> 27.7 us
    pallas_call x1, Pallas kernels: 9.08 us -> 1.63 us  [hand_over(): pl.pallas_call(copies, out_shape=[jax.ShapeDtypeStruct(field.shape, field...]
    pallas_call x1, Pallas kernels: 27.7 us -> 26.1 us  [body(): pl.pallas_call(functools.partial(kernel, stages, devs, total), out_shape=...]
where the time goes in v2:
time: 28.5 us; the launch traced here: 28.3 us
  Pallas kernels  27.7 us (97%)
  between operations  0.64 us (2%)
    pallas_call x1, Pallas kernels, body(): pl.pallas_call(functools.partial(kernel, stages, devs, total), out_shape=...  26.1 us
    pallas_call x1, Pallas kernels, hand_over(): pl.pallas_call(copies, out_shape=[jax.ShapeDtypeStruct(field.shape, field...  1.63 us

profile of v2, /device:TPU:0, one launch (start us, length us, event | category | flops | bytes accessed | tf_op | source)
XLA Modules:
  0.0 28.3 jit_solution(11530739397568908832)
XLA Ops:
  0.6 26.1 %shard_map.68 = (f32[2,32,512]{2,1,0:T(8,128)}, f32[2,32,512]{2,1,0:T(8,128)}) custom-call(s32[64]{0:T(128)} %lengths_hbm.1, f32[2,32,512]{2,1,0:T(8,128)} %forces_hbm.1, f32[2,512]{1,0:T(2,128)} %weights_hbm.1, s32[2,512]{1,0:T(2,128)} %order_hbm.1, bf16[2,1024,1024]{2,1,0:T(8,128)(2,1)} %operators_ref.1), custom_call_target="tpu_custom_call" | custom-call | flops 805306368 | bytes 4718592 | tf_op jit(solution)/shard_map/pallas_call | solution.py:419
  26.7 1.6 %shard_map.69 = (f32[2,32,512]{2,1,0:T(8,128)}, f32[2,32,512]{2,1,0:T(8,128)}) custom-call(f32[2,32,512]{2,1,0:T(8,128)} %get-tuple-element.4.refs_0_, f32[2,32,512]{2,1,0:T(8,128)} %get-tuple-element.5.refs_1_), custom_call_target="tpu_custom_call" | custom-call | tf_op jit(solution)/shard_map/pallas_call | solution.py:399

commit v3 on v2

--- a/solution.py
+++ b/solution.py
@@ -59,6 +59,27 @@
 def small_tn(x, y):
     return lax.dot_general(
         x, y, (((0,), (0,)), ((), ())), precision=EXACT, preferred_element_type=F32
+    )
+
+
+def pair(x):
+    return jnp.concatenate(split(x), axis=0)
+
+
+def cross(first, second):
+    size = first.shape[0] // 2
+    four = dot_nt(first, second)
+    both = four[:size] + four[size:]
+    return both[:, :size] + both[:, size:]
+
+
+def mix(matrix, field):
+    high, low = split(matrix)
+    field_high, field_low = split(field)
+    return lax.dot_general(
+        jnp.concatenate([high, low, high], axis=0),
+        jnp.concatenate([field_high, field_high, field_low], axis=0),
+        (((0,), (0,)), ((), ())), preferred_element_type=F32,
     )
 
 
@@ -108,10 +129,10 @@
 
 def kernel(stages, devs, total, lengths_hbm, forces_hbm, weights_hbm, order_hbm, operators_ref,
            solution_ref, residual_ref,
-           lengths_ref, forces_ref, weights_ref, order_ref, ops, pick, start, search, image, remainder, scaled, second, following, product, applied,
+           lengths_ref, forces_ref, weights_ref, order_ref, ops, pick, start, search, image, remainder, scaled, second, following, base, product, applied,
            fwd_src, fwd_dst, fwdlow_src, fwdlow_dst, right_src, right_dst, ret_src, ret_dst, retlow_src, retlow_dst,
            ret2_src, ret2_dst, sums_src, sums_dst, last_src, last_dst,
-           ops_sem, small_sem, halo_send, halo_recv, sums_send, sums_recv, last_send, last_recv):
+           ops_sem, small_sem, out_sem, halo_send, halo_recv, sums_send, sums_recv, last_send, last_recv):
     number, loads, breadth = forces_ref.shape
     grp, dev = lax.axis_index("grp"), lax.axis_index("dev")
     me = grp * devs + dev
@@ -222,15 +243,13 @@
     for l in range(1, last):
         apply(l, [turned[l - 1], stacks[l]], product)
     product[0] = dot(stacks[0], ops[0, breadth:, :])
-    def whole(pair):
-        return pair[:loads].astype(F32) + pair[loads:].astype(F32)
-
     projection = curvature = 0.0
     for l in range(number):
-        projection = projection + dot_nt(search[l], start[l], EXACT)
+        projection = projection + cross(stacks[l], pair(start[l]))
         if l > 0:
-            curvature = curvature + dot_nt(search[l], product[l, :loads, breadth:], EXACT)
-            curvature = curvature + dot_nt(whole(turned[l - 1]), product[l, :loads, :breadth], EXACT)
+            curvature = curvature + cross(
+                jnp.concatenate([turned[l - 1], stacks[l]], axis=1), pair(product[l, :loads, :])
+            )
 
     def finish_image(l, left):
         image[l] = jnp.where(masks[l], product[l, :loads, breadth:] + gather(l, left), 0.0)
@@ -263,10 +282,8 @@
     start_if(has_prev, back)
     product[0, :loads, breadth:] += dot(fwd_dst[...], ops[0, :breadth, breadth:])
     arrived(has_prev, forward_low, fwdlow_dst)
-    curvature = curvature + dot_nt(search[0], product[0, :loads, breadth:], EXACT)
-    curvature = curvature + dot_nt(
-        fwd_dst[...].astype(F32) + fwdlow_dst[:loads].astype(F32), owed, EXACT
-    )
+    arriving = jnp.concatenate([fwd_dst[...], fwdlow_dst[:loads]], axis=0)
+    curvature = curvature + cross(arriving, pair(owed)) + cross(stacks[0], pair(product[0, :loads, breadth:]))
     tall = pack(curvature).shape[0]
     sums_src[0] = jnp.concatenate([pack(curvature), pack(projection)], axis=0)
     pending = [exchange(0, sums_src, sums_dst, sums_send, sums_recv)]
@@ -275,7 +292,7 @@
     for l in range(last):
         finish_image(l, product[l + 1, :loads, :breadth])
         turned[l] = dot(stacks[l], pick[l]).astype(BF16)
-        middle = middle + dot_nt(scaled[l], image[l], EXACT)
+        middle = middle + cross(stacks[l], pair(image[l]))
 
     arrived(has_prev, forward_right, right_dst)
     incoming = positions < jnp.where(has_prev, lengths_ref[jnp.maximum(me * number - 1, 0)], 0)
@@ -285,10 +302,10 @@
     )[:1]
     across_scaled = turned_weights * across
     across_stack = jnp.concatenate(split(across_scaled), axis=0)
-    middle = middle + dot_nt(across_scaled, across, EXACT)
-
-    def energy(pair, values):
-        return dot_nt(whole(pair), values[:loads] + values[loads:], EXACT)
+    middle = middle + cross(across_stack, pair(across))
+
+    def energy(field, values):
+        return cross(field, pair(values[:loads] + values[loads:]))
 
     apply(0, [across_stack, stacks[0]], applied)
     ret2_src[...] = applied[0, :loads, :breadth] + applied[0, loads:, :breadth]
@@ -343,10 +360,10 @@
         remainder[l] = jnp.where(masks[l], product[l, loads:, breadth:] + dot_nt(left_low, pick[l]), 0.0)
         second[l] = jnp.where(masks[l], right + gather(l, left), 0.0)
     for l in range(number):
-        solution_ref[l] = small_tn(alpha, search[l])
-        residual_ref[l] = start[l] - small_tn(alpha, image[l])
-        following[l] = small_tn(alpha, scaled[l])
-        second[l] = small_tn(alpha, second[l])
+        base[0, l] = mix(alpha, search[l])
+        base[1, l] = start[l] - mix(alpha, image[l])
+        following[l] = mix(alpha, scaled[l])
+        second[l] = mix(alpha, second[l])
         image[l] += remainder[l]
     summed = collect(len(stages) - 1, trailing[-1], last_src, last_dst)
     middle, outer = unpack(summed[:tall], loads), unpack(summed[tall:], loads)
@@ -355,9 +372,15 @@
     shift = small(inverse, carried)
     again = small_tn(alpha, small(outer, alpha) - small(middle, shift))
     alpha2 = eliminate(again, small_tn(alpha, carried - curvature))
+    leaving = []
     for l in range(number):
-        solution_ref[l] += small_tn(alpha2, small_tn(shift, search[l]) - following[l])
-        residual_ref[l] -= small_tn(alpha2, small_tn(shift, image[l]) - second[l])
+        base[0, l] += mix(alpha2, mix(shift, search[l]) - following[l])
+        leaving.append(pltpu.make_async_copy(base.at[0, l], solution_ref.at[l], out_sem.at[0, l]))
+        leaving[-1].start()
+    for l in range(number):
+        base[1, l] -= mix(alpha2, mix(shift, image[l]) - second[l])
+        leaving.append(pltpu.make_async_copy(base.at[1, l], residual_ref.at[l], out_sem.at[1, l]))
+        leaving[-1].start()
 
     @pl.when(has_next)
     def _():
@@ -369,6 +392,8 @@
         for copy in (back, back_low, back_second):
             copy.wait_send()
 
+    for copy in leaving:
+        copy.wait()
     for copies in pending + trailing:
         for copy in copies:
             copy.wait_send()
@@ -415,12 +440,11 @@
     tall, wide = jax.eval_shape(pack, jax.ShapeDtypeStruct((loads, loads), F32)).shape
     boxes = sum(stage[0] - 1 for stage in stages)
     field = pltpu.VMEM(forces.shape, F32)
-    vmem = pl.BlockSpec(memory_space=pltpu.VMEM)
     results = pl.pallas_call(
         functools.partial(kernel, stages, devs, total),
         out_shape=[jax.ShapeDtypeStruct(forces.shape, F32)] * 2,
         in_specs=[pl.BlockSpec(memory_space=pl.ANY)] * 5,
-        out_specs=[vmem, vmem],
+        out_specs=[pl.BlockSpec(memory_space=pl.ANY)] * 2,
         scratch_shapes=[
             pltpu.SMEM(lengths.shape, jnp.int32),
             field,
@@ -429,6 +453,7 @@
             pltpu.VMEM(operators.shape, BF16),
             pltpu.VMEM((number, breadth, breadth), BF16),
             field, field, field, field, field, field, field,
+            pltpu.VMEM((2,) + forces.shape, F32),
             pltpu.VMEM((number, 2 * loads, 2 * breadth), F32),
             pltpu.VMEM((number, 2 * loads, 2 * breadth), F32),
             pltpu.VMEM((loads, breadth), BF16),
@@ -449,6 +474,7 @@
             pltpu.VMEM((boxes, 2 * tall, wide), F32),
             pltpu.SemaphoreType.DMA((number,)),
             pltpu.SemaphoreType.DMA((4,)),
+            pltpu.SemaphoreType.DMA((2, number)),
             pltpu.SemaphoreType.DMA((6,)),
             pltpu.SemaphoreType.DMA((6,)),
             pltpu.SemaphoreType.DMA((boxes,)),

time: 28.5 us -> 28 us (0.982)
  Pallas kernels: 27.7 us -> 27.2 us
    pallas_call x1, Pallas kernels: 26.1 us -> 25.6 us  [body(): pl.pallas_call(functools.partial(kernel, stages, devs, total), out_shape=...]
where the time goes in v3:
time: 28 us; the launch traced here: 27.9 us
  Pallas kernels  27.2 us (97%)
  between operations  0.64 us (2%)
    pallas_call x1, Pallas kernels, body(): pl.pallas_call(functools.partial(kernel, stages, devs, total), out_shape=...  25.6 us
    pallas_call x1, Pallas kernels, hand_over(): pl.pallas_call(copies, out_shape=[jax.ShapeDtypeStruct(field.shape, field...  1.63 us

profile of v3, /device:TPU:0, one launch (start us, length us, event | category | flops | bytes accessed | tf_op | source)
XLA Modules:
  0.0 27.9 jit_solution(4701739701052694596)
XLA Ops:
  0.6 25.6 %shard_map.68 = (f32[2,32,512]{2,1,0:T(8,128)}, f32[2,32,512]{2,1,0:T(8,128)}) custom-call(s32[64]{0:T(128)} %lengths_hbm.1, f32[2,32,512]{2,1,0:T(8,128)} %forces_hbm.1, f32[2,512]{1,0:T(2,128)} %weights_hbm.1, s32[2,512]{1,0:T(2,128)} %order_hbm.1, bf16[2,1024,1024]{2,1,0:T(8,128)(2,1)} %operators_ref.1), custom_call_target="tpu_custom_call" | custom-call | flops 805306368 | bytes 4718592 | tf_op jit(solution)/shard_map/pallas_call | solution.py:443
  26.2 1.6 %shard_map.69 = (f32[2,32,512]{2,1,0:T(8,128)}, f32[2,32,512]{2,1,0:T(8,128)}) custom-call(f32[2,32,512]{2,1,0:T(8,128)} %get-tuple-element.4.refs_0_, f32[2,32,512]{2,1,0:T(8,128)} %get-tuple-element.5.refs_1_), custom_call_target="tpu_custom_call" | custom-call | tf_op jit(solution)/shard_map/pallas_call | solution.py:424
